TPU v7x, 32 devices: a whole 2x2x4 slice. The times are simulated.
32 devices in a mesh: expert: 4 (over y, x), tensor: 4 (over z), dp: 2 (over core).
Axes of the slice: x: 2, y: 2, z: 4, core: 2. Of those that a mesh axis runs over, the one named last changes fastest.
Arguments:
- out_grad: bfloat16 [4096, 2048], P(('expert', 'dp'), 'tensor'), may hold values from -1.5 to 1.5
- expert_ids: int32 [4096, 2], P(('expert', 'dp')), may hold values from 0 to 31, all different within a row; in each aligned block of 512 rows (0 to 511, 512 to 1023, ...) at most 36 rows name the same one
- gate_weights: float32 [4096, 2], P(('expert', 'dp')), may hold values from 0.05 to 1
- keep: int32 [4096, 2], P(('expert', 'dp')), may hold values 0 or 1
- hidden_act: bfloat16 [32, 288, 7168], P('expert', 'dp', 'tensor'), may hold values from -3 to 3
- down_weight: bfloat16 [32, 7168, 2048], P('expert', 'tensor', 'dp'), may hold values from -0.0625 to 0.0625
Outputs:
- grad_down: bfloat16 [32, 7168, 2048], P('expert', 'tensor', 'dp')
- grad_hidden: bfloat16 [32, 288, 7168], P('expert', 'dp', 'tensor')
- gate_grad: float32 [4096, 2], P(('expert', 'dp'))
Inputs may be any that keep to these rules, and one draw needn't show every extreme that they name: `expert_ids`: each row names two different experts; among the 512 rows of one device no expert is named more than 36 times, and in every draw some device names some expert exactly 36 times.
All inputs are finite; a program needn't handle non-finite values. No bound on the sum of `keep` on one device may be relied on, other than what follows from the above.
Results may differ from a plain program's by a relative error of at most 0.0064.
Values may be sent and summed in bfloat16 or wider, within the bound.
A program may use at most 256 MiB of HBM per device.

v0:
```python
import jax
import jax.numpy as jnp
from jax import lax
from jax.sharding import PartitionSpec as P


def from_partner(value, axis, stride):
    mask = 2**stride
    pairs = [(source, source ^ mask) for source in range(lax.axis_size(axis))]
    return lax.ppermute(value, axis, pairs)


def body(out_grad, expert_ids, gate_weights, keep, hidden_act, down_weight):
    token_count = out_grad.shape[0]
    experts = lax.axis_size("expert")
    local_experts = hidden_act.shape[0]
    total_experts = experts * local_experts
    slot_count = hidden_act.shape[1]
    capacity = slot_count // experts
    chosen = expert_ids.reshape(-1)
    onehot = (chosen[:, None] == jnp.arange(total_experts, dtype=jnp.int32)[None, :]).astype(
        jnp.int32
    )
    ranking = jnp.cumsum(onehot, axis=0) - onehot
    position = chosen * capacity + jnp.sum(ranking * onehot, axis=1)
    placing = (
        position[None, :] == jnp.arange(total_experts * capacity, dtype=jnp.int32)[:, None]
    ).astype(jnp.bfloat16)
    kept_mask = keep.reshape(-1).astype(jnp.float32)
    scale_flat = (gate_weights.reshape(-1) * kept_mask).astype(jnp.bfloat16)
    slot_scale = (
        jnp.dot(placing, scale_flat[:, None], preferred_element_type=jnp.float32)
        .astype(jnp.bfloat16)
        .reshape(experts, local_experts, capacity)
    )
    gathered = lax.all_gather(out_grad, "tensor", axis=1, tiled=True)
    outgoing = jnp.dot(
        placing, jnp.repeat(gathered, 2, axis=0), preferred_element_type=jnp.float32
    ).astype(jnp.bfloat16)
    arrived, arrived_scale = (
        lax.all_to_all(
            outgoing.reshape(experts, local_experts, capacity, -1),
            "expert",
            split_axis=0,
            concat_axis=2,
            tiled=True,
        ),
        lax.all_to_all(slot_scale, "expert", split_axis=0, concat_axis=2, tiled=True),
    )
    routed = arrived.reshape(local_experts, slot_count, -1)
    weight = arrived_scale.reshape(local_experts, slot_count).astype(jnp.float32)
    backprop = lax.dot_general(
        routed,
        lax.all_gather(down_weight, "dp", axis=2, tiled=True),
        (((2,), (2,)), ((0,), (0,))),
        preferred_element_type=jnp.float32,
    )
    grad_hidden = (weight[:, :, None] * backprop).astype(jnp.bfloat16)
    partial_score = jnp.sum(backprop * hidden_act.astype(jnp.float32), axis=2)
    scores = lax.psum(partial_score, "tensor")
    returned = lax.all_to_all(
        scores.reshape(local_experts, experts, capacity),
        "expert",
        split_axis=1,
        concat_axis=0,
        tiled=True,
    )
    gate_grad = (jnp.take(returned.reshape(-1), position) * kept_mask).reshape(token_count, 2)
    scaled = (weight[:, :, None] * routed.astype(jnp.float32)).astype(jnp.bfloat16)
    contract_rows = (((1,), (1,)), ((0,), (0,)))
    half_width = scaled.shape[2] // 2
    dp_index = lax.axis_index("dp")
    own_cols = lax.dynamic_slice_in_dim(scaled, dp_index * half_width, half_width, 2)
    theirs = lax.dynamic_slice_in_dim(scaled, (1 - dp_index) * half_width, half_width, 2)
    peer_hidden, peer_scaled = from_partner((hidden_act, theirs), "dp", 0)
    own_term = lax.dot_general(
        hidden_act, own_cols, contract_rows, preferred_element_type=jnp.float32
    ).astype(jnp.bfloat16)
    peer_term = lax.dot_general(
        peer_hidden, peer_scaled, contract_rows, preferred_element_type=jnp.float32
    ).astype(jnp.bfloat16)
    own_term, peer_term = lax.optimization_barrier((own_term, peer_term))
    summed = own_term.astype(jnp.float32) + peer_term.astype(jnp.float32)
    grad_down = summed.astype(jnp.bfloat16)
    return (grad_down, grad_hidden, gate_grad)


def solution(mesh):
    in_specs = (
        P(("expert", "dp"), "tensor"),
        P(("expert", "dp"), None),
        P(("expert", "dp"), None),
        P(("expert", "dp"), None),
        P("expert", "dp", "tensor"),
        P("expert", "tensor", "dp"),
    )
    out_specs = (
        P("expert", "tensor", "dp"),
        P("expert", "dp", "tensor"),
        P(("expert", "dp"), None),
    )
    return jax.shard_map(body, mesh=mesh, in_specs=in_specs, out_specs=out_specs, check_vma=False)
```

profile of v0, /device:TPU:0, one launch (start us, length us, event | category | flops | bytes accessed | tf_op | source)
XLA Modules:
  0.0 334.6 jit_solution(5051636385490135882)
XLA Ops:
  7.2 0.7 all-gather.3.cloned.1.call-update
  8.0 0.7 all-gather.5.cloned.1.call-update
  9.2 9.0 %reduce-window.6 = s32[32,8,128]{2,1,0:T(8,128)S(1)} reduce-window(s32[32,8,128]{2,1,0:T(8,128)S(1)} %fusion.10, s32[]{:T(128)} %constant.12.clone.1), window={size=1x1x128 pad=0_0x0_0x127_0}, to_apply=%region_0.0 | reduce-window | flops 4161536 | bytes 262148 | tf_op jit(solution)/shard_map/reduce-window
  18.9 0.2 reshape.134
  19.3 0.9 fusion.6
  20.3 0.7 reshape.138
  21.0 5.2 %all-to-all-start = ((bf16[4,2,144]{2,1,0:T(2,128)(2,1)}), bf16[4,2,144]{2,1,0:T(2,128)(2,1)S(1)}, u32[]{:S(2)}, u32[]{:S(2)}) async-start(bf16[4,2,144]{2,1,0:T(2,128)(2,1)} %reshape.138), calls=%async_computation | async-start | bytes 8192 | tf_op jit(solution)/shard_map/all_to_all | solution.py:48
  26.1 32.1 %all-gather.3.cloned.1.call-done = bf16[512,2048]{1,0:T(8,128)(2,1)} async-done(((bf16[512,512]{1,0:T(8,128)(2,1)}), bf16[512,2048]{1,0:T(8,128)(2,1)}) %all-gather.3.cloned.1.call-update) | async-done | bytes 2097168 | tf_op jit(solution)/shard_map/all_gather | solution.py:36
  58.2 5.4 %broadcast_in_dim.6 = bf16[512,2,2048]{2,1,0:T(2,128)(2,1)} broadcast(bf16[512,2048]{1,0:T(8,128)(2,1)} %all-gather.3.cloned.1.call-done), dimensions={0,2} | broadcast | bytes 6291456 | tf_op jit(solution)/shard_map/broadcast_in_dim | solution.py:38
  63.6 7.9 %reshape.119 = bf16[1024,2048]{1,0:T(8,128)(2,1)} reshape(bf16[512,2,2048]{2,1,0:T(2,128)(2,1)} %broadcast_in_dim.6) | data formatting | bytes 8388608 | tf_op jit(solution)/shard_map/reshape | solution.py:38
  71.5 10.9 %convolution_convert_fusion = bf16[1152,2048]{1,0:T(8,128)(2,1)} fusion(bf16[1024,2048]{1,0:T(8,128)(2,1)} %reshape.119, s32[1024]{0:T(1024)S(1)} %multiply_add_fusion), kind=kOutput, calls=%fused_computation.7 | convolution fusion | flops 4835377152 | bytes 8916992 | tf_op jit(solution)/shard_map/dot_general | solution.py:37
  82.4 8.3 %reshape.120 = bf16[4,8,36,2048]{3,2,1,0:T(8,128)(2,1)} reshape(bf16[1152,2048]{1,0:T(8,128)(2,1)} %convolution_convert_fusion) | data formatting | bytes 9437184 | tf_op jit(solution)/shard_map/reshape | solution.py:42
  90.7 9.8 %copy.44 = bf16[4,8,36,2048]{3,1,2,0:T(8,128)(2,1)} copy(bf16[4,8,36,2048]{3,2,1,0:T(8,128)(2,1)} %reshape.120) | data formatting | bytes 9437184 | tf_op jit(solution)/shard_map/reshape | solution.py:42
  100.5 5.5 %all-to-all-start.1 = ((bf16[4,8,36,2048]{3,1,2,0:T(8,128)(2,1)}), bf16[4,8,36,2048]{3,1,2,0:T(8,128)(2,1)}, u32[]{:S(2)}, u32[]{:S(2)}) async-start(bf16[4,8,36,2048]{3,1,2,0:T(8,128)(2,1)} %copy.44), calls=%async_computation.1 | async-start | bytes 9437184 | tf_op jit(solution)/shard_map/all_to_all | solution.py:41
  106.2 52.2 %all-to-all-done.1 = bf16[4,8,36,2048]{3,1,2,0:T(8,128)(2,1)} async-done(((bf16[4,8,36,2048]{3,1,2,0:T(8,128)(2,1)}), bf16[4,8,36,2048]{3,1,2,0:T(8,128)(2,1)}, u32[]{:S(2)}, u32[]{:S(2)}) %all-to-all-start.1) | async-done | bytes 4718624 | tf_op jit(solution)/shard_map/all_to_all | solution.py:41
  158.4 5.6 %multiply_convert_fusion = bf16[8,144,2048]{2,1,0:T(8,128)(2,1)S(1)} fusion(f32[8,144]{1,0:T(8,128)S(1)} %reshape.124, bf16[8,144,2048]{2,0,1:T(8,128)(2,1)} %bitcast.6), kind=kLoop, calls=%fused_computation.4 | loop fusion | flops 7077888 | bytes 9441792 | tf_op jit(solution)/shard_map/convert_element_type | solution.py:69
  164.0 2.2 copy-done
  166.2 1.7 constant_dynamic-slice_fusion
  167.9 0.2 reduce_sum.23
  168.3 14.9 %convert_bitcast_fusion.1 = bf16[8,1792,1024]{1,2,0:T(8,128)(2,1)} fusion(bf16[8,144,1792]{2,1,0:T(8,128)(2,1)} %param.10, bf16[8,144,2048]{2,1,0:T(8,128)(2,1)} %copy-done, s32[]{:T(128)S(6)} %select_n.28), kind=kOutput, calls=%fused_computation.3 | convolution fusion | flops 4242538496 | bytes 35848196 | tf_op jit(solution)/shard_map/dot_general | solution.py:76
  183.3 14.9 %convert_bitcast_fusion = bf16[8,1792,1024]{1,2,0:T(8,128)(2,1)} fusion(bf16[8,144,1024]{2,1,0:T(8,128)(2,1)S(1)} %collective-permute-done, bf16[8,144,1792]{2,1,0:T(8,128)(2,1)} %collective-permute-done.1), kind=kOutput, calls=%fused_computation.2 | convolution fusion | flops 4242538496 | bytes 35848192 | tf_op jit(solution)/shard_map/dot_general | solution.py:79
  198.2 34.8 %multiply_reduce_fusion = (f32[8,144]{1,0:T(8,128)S(1)}, bf16[8,144,1792]{2,1,0:T(8,128)(2,1)}) fusion(bf16[8,144,1792]{2,1,0:T(8,128)(2,1)} %param.10, f32[8,144]{1,0:T(8,128)S(1)} %reshape.124, bf16[8,1792,2048]{2,1,0:T(8,128)(2,1)} %all-gather.5.cloned.1.call-done, bf16[8,144,2048]{2,0,1:T(8,128)(2,1)} %bitcast.6), kind=kOutput, calls=%fused_computation.5 | convolution fusion | flops 8466037760 | bytes 71705600 | tf_op jit(solution)/shard_map/dot_general | solution.py:52
  233.1 16.9 %psum.7 = f32[8,4,36]{2,1,0:T(4,128)S(1)} all-reduce(f32[8,4,36]{2,1,0:T(4,128)S(1)} %reshape.122), channel_id=1, replica_groups=mesh['expert'=4,'tensor'=4,'dp'=2] {'tensor'}, use_global_device_ids=true, to_apply=%region_4.5 | all-reduce | flops 1152 | bytes 9216 | tf_op jit(solution)/shard_map/psum | solution.py:60
  250.0 0.7 reshape.140
  250.7 3.2 all-to-all-start.2
  253.9 29.4 %add_convert_fusion = bf16[8,1792,1024]{1,2,0:T(8,128)(2,1)} fusion(bf16[8,1792,1024]{1,2,0:T(8,128)(2,1)} %convert_bitcast_fusion, bf16[8,1792,1024]{1,2,0:T(8,128)(2,1)} %convert_bitcast_fusion.1), kind=kLoop, calls=%fused_computation.1 | loop fusion | flops 58720256 | bytes 88080384 | tf_op jit(solution)/shard_map/convert_element_type | solution.py:84
  283.3 35.9 %copy.49 = bf16[8,1792,1024]{2,1,0:T(8,128)(2,1)} copy(bf16[8,1792,1024]{1,2,0:T(8,128)(2,1)} %add_convert_fusion) | data formatting | bytes 58720256
  319.2 0.5 broadcast.68
  319.7 0.7 reduce.2
  320.6 6.2 %gather_fusion = f32[1024]{0:T(1024)S(1)} fusion(f32[1152]{0:T(1024)S(1)} %reshape.123, s32[1024]{0:T(1024)S(1)} %broadcast_clamp_fusion), kind=kCustom, calls=%fused_computation | custom fusion | bytes 12288 | tf_op jit(solution)/shard_map/jit(_take)/gather | solution.py:68
  326.7 0.2 gather.7
  327.1 0.7 copy.50
  (46 shorter events, 2.4 us)
Async XLA Ops:
  7.2 51.0 %all-gather.3.cloned.1.call-start = ((), (), s32[]{:S(2)}) async-start(), calls=%async_computation.3 | async-start | bytes 2621440 | tf_op jit(solution)/shard_map/all_gather | solution.py:36
  7.9 0.8 copy-start.1
  7.9 10.7 %copy-start.2 = (s32[512,2]{0,1:T(2,128)S(1)}, s32[512,2]{0,1:T(2,128)}, u32[]{:S(2)}) copy-start(s32[512,2]{0,1:T(2,128)} %param.9) | copy-start | bytes 12292
  7.9 10.8 %copy-start.3 = (f32[512,2]{0,1:T(2,128)S(1)}, f32[512,2]{0,1:T(2,128)}, u32[]{:S(2)}) copy-start(f32[512,2]{0,1:T(2,128)} %param.8) | copy-start | bytes 12292
  7.9 190.3 %all-gather.5.cloned.1.call-start = ((), (), s32[]{:S(2)}) async-start(), calls=%async_computation.4 | async-start | bytes 88080384 | tf_op jit(solution)/shard_map/all_gather | solution.py:54
  21.0 79.5 %all-to-all-start = ((bf16[4,2,144]{2,1,0:T(2,128)(2,1)}), bf16[4,2,144]{2,1,0:T(2,128)(2,1)S(1)}, u32[]{:S(2)}, u32[]{:S(2)}) async-start(bf16[4,2,144]{2,1,0:T(2,128)(2,1)} %reshape.138), calls=%async_computation | async-start | bytes 8192 | tf_op jit(solution)/shard_map/all_to_all | solution.py:48
  100.5 57.9 %all-to-all-start.1 = ((bf16[4,8,36,2048]{3,1,2,0:T(8,128)(2,1)}), bf16[4,8,36,2048]{3,1,2,0:T(8,128)(2,1)}, u32[]{:S(2)}, u32[]{:S(2)}) async-start(bf16[4,8,36,2048]{3,1,2,0:T(8,128)(2,1)} %copy.44), calls=%async_computation.1 | async-start | bytes 9437184 | tf_op jit(solution)/shard_map/all_to_all | solution.py:41
  106.0 77.3 %collective-permute-start.1 = (bf16[8,144,1792]{2,1,0:T(8,128)(2,1)}, bf16[8,144,1792]{2,1,0:T(8,128)(2,1)}, u32[]{:S(2)}, u32[]{:S(2)}) collective-permute-start(bf16[8,144,1792]{2,1,0:T(8,128)(2,1)} %param.10), channel_id=1, source_target_pairs={{0,1},{1,0},{2,3},{3,2},{4,5},{5,4},{6,7},{7,6},{8,9},{9,8},{10,11... | collective-permute-start | bytes 12386312 | tf_op jit(solution)/shard_map/ppermute | solution.py:10
  164.0 2.2 copy-start
  167.9 15.4 %collective-permute-start = (bf16[8,144,1024]{2,1,0:T(8,128)(2,1)}, bf16[8,144,1024]{2,1,0:T(8,128)(2,1)S(1)}, u32[]{:S(2)}, u32[]{:S(2)}) collective-permute-start(bf16[8,144,1024]{2,1,0:T(8,128)(2,1)} %constant_dynamic-slice_fusion), channel_id=1, source_target_pairs={{0,1},{1,0},{2,3},{3,2},{4,5},{5,4},{6,7},{7,6},{8,9},{9,8},{10,11... | collective-permute-start | bytes 7077896 | tf_op jit(solution)/shard_map/ppermute | solution.py:10
  250.7 68.5 %all-to-all-start.2 = ((f32[4,1,288]{2,1,0:T(1,128)}), f32[4,1,288]{2,1,0:T(1,128)S(1)}, u32[]{:S(2)}, u32[]{:S(2)}) async-start(f32[4,1,288]{2,1,0:T(1,128)} %reshape.140), calls=%async_computation.2 | async-start | bytes 12288 | tf_op jit(solution)/shard_map/all_to_all | solution.py:61
Sparse Core Ops, SparseCore 0:
  9.6 48.5 all-gather.2
  59.7 88.8 all-gather.4
where the time goes:
time: 336 us; the launch traced here: 335 us
  waiting for transfers between devices  85.6 us (25%)
  local copies, waits for them, and re-layouts  82.3 us (24%)
  matrix products  76.5 us (23%)
  other arithmetic  45 us (13%)
  blocking collectives  16.9 us (5%)
  between operations  14.3 us (4%)
  starting transfers between devices  14 us (4%)
    all_to_all x1, waiting for transfers between devices, body(): lax.all_to_all(outgoing.reshape(experts, local_experts, capacity, -1), 'e...  52.2 us
    unnamed x17, local copies, waits for them, and re-layouts  40.7 us
    dot_general x1, matrix products, body(): lax.dot_general(routed, lax.all_gather(down_weight, 'dp', axis=2, tiled=T...  34.8 us
    all_gather x1, waiting for transfers between devices, body(): gathered = lax.all_gather(out_grad, 'tensor', axis=1, tiled=True)  32.1 us
    convert_element_type x1, other arithmetic, body(): grad_down = summed.astype(jnp.bfloat16)  29.4 us
    reshape x2, local copies, waits for them, and re-layouts, body(): outgoing.reshape(experts, local_experts, capacity, -1)  18.1 us
    psum x1, blocking collectives, body(): scores = lax.psum(partial_score, 'tensor')  16.9 us
    dot_general x1, matrix products, body(): lax.dot_general(peer_hidden, peer_scaled, contract_rows, preferred_elemen...  14.9 us
  transfers between devices with their start and end apart: 7, of which 2 were waited for; matrix products, arithmetic and copies ran while one was open for 47% of the time, Pallas kernels for 0%

commit v1 on v0

v1 whole, which is shorter than its diff:
```python
import functools

import jax
import jax.numpy as jnp
from jax import lax
from jax.experimental import pallas as pl
from jax.experimental.pallas import tpu as pltpu
from jax.sharding import PartitionSpec as P

CHUNKS = 1
VMEM_LIMIT = 56 * 1024 * 1024


def swap(value):
    return lax.ppermute(value, "dp", [(0, 1), (1, 0)])


def gather_rows(own_refs, peer_refs, rows, shards):
    slots = own_refs[0].shape[1]
    chunks = len(own_refs)
    part = own_refs[0].shape[2] // shards
    for c in range(chunks):
        for s in range(shards):
            to = pl.ds((s * chunks + c) * part, part)
            at = pl.ds(s * part, part)
            rows[pl.ds(0, slots), to] = own_refs[c][0, :, at]
            rows[pl.ds(slots, slots), to] = peer_refs[c][0, :, at]


def backprop_kernel(chunks, shards, *refs):
    own, peer = refs[:chunks], refs[chunks : 2 * chunks]
    own_w, peer_w, own_h, peer_h, weight, own_out, peer_out, score, rows = refs[2 * chunks :]
    slots = own_h.shape[1]
    gather_rows(own, peer, rows, shards)
    back = lax.dot_general(
        rows[...], weight[0], (((1,), (1,)), ((), ())), preferred_element_type=jnp.float32
    )
    mine, theirs = back[:slots], back[slots:]
    own_out[0] = (own_w[0] * mine).astype(jnp.bfloat16)
    peer_out[0] = (peer_w[0] * theirs).astype(jnp.bfloat16)
    score[0, pl.ds(0, slots), :] = jnp.sum(
        mine * own_h[0].astype(jnp.float32), axis=1, keepdims=True
    )
    score[0, pl.ds(slots, slots), :] = jnp.sum(
        theirs * peer_h[0].astype(jnp.float32), axis=1, keepdims=True
    )


def grad_kernel(chunks, shards, *refs):
    own, peer = refs[:chunks], refs[chunks : 2 * chunks]
    own_w, peer_w, own_h, peer_h, out, rows, hidden = refs[2 * chunks :]
    slots = own_h.shape[1]
    gather_rows(own, peer, rows, shards)
    for first, weight, source in ((0, own_w, own_h), (slots, peer_w, peer_h)):
        at = pl.ds(first, slots)
        rows[at, :] = (weight[0] * rows[at, :].astype(jnp.float32)).astype(jnp.bfloat16)
        hidden[at, :] = source[0]
    out[0] = lax.dot_general(
        hidden[...], rows[...], (((0,), (0,)), ((), ())), preferred_element_type=jnp.float32
    ).astype(jnp.bfloat16)


def per_expert(array):
    return pl.BlockSpec((1,) + array.shape[1:], lambda e: (e, 0, 0))


def call(kernel, inputs, outputs, scratch, flops):
    moved = sum(a.size * a.dtype.itemsize for a in (*inputs, *outputs))
    return pl.pallas_call(
        kernel,
        grid=(inputs[0].shape[0],),
        in_specs=[per_expert(a) for a in inputs],
        out_specs=[per_expert(a) for a in outputs],
        out_shape=outputs,
        scratch_shapes=scratch,
        compiler_params=pltpu.CompilerParams(vmem_limit_bytes=VMEM_LIMIT),
        cost_estimate=pl.CostEstimate(flops=flops, bytes_accessed=moved, transcendentals=0),
    )(*inputs)


def body(out_grad, expert_ids, gate_weights, keep, hidden_act, down_weight):
    token_count, shard = out_grad.shape
    experts = lax.axis_size("expert")
    tensor = lax.axis_size("tensor")
    local, slots, units = hidden_act.shape
    half = down_weight.shape[2]
    capacity = slots // experts
    total = experts * local * capacity
    dp_index = lax.axis_index("dp")
    peer_h = swap(hidden_act)

    chosen = expert_ids.reshape(-1)
    order = jnp.arange(chosen.shape[0], dtype=jnp.int32)
    earlier = (chosen[:, None] == chosen[None, :]) & (order[None, :] < order[:, None])
    slot = jnp.sum(earlier.astype(jnp.int32), axis=1)
    position = (chosen // local) * (capacity * local) + slot * local + chosen % local
    pair = position.reshape(token_count, 2)
    places = jnp.arange(total, dtype=jnp.int32)
    placing = (
        (places[:, None] == pair[:, 0][None, :]) | (places[:, None] == pair[:, 1][None, :])
    ).astype(jnp.bfloat16)
    kept_mask = keep.reshape(-1).astype(jnp.float32)
    scale_flat = (gate_weights.reshape(-1) * kept_mask).astype(jnp.bfloat16).astype(jnp.float32)
    hit = places[:, None] == position[None, :]
    slot_scale = jnp.sum(jnp.where(hit, scale_flat[None, :], 0.0), axis=1)
    own_w = lax.all_to_all(
        slot_scale.reshape(experts, capacity * local), "expert", 0, 0, tiled=True
    )
    own_w = own_w.reshape(slots, local).T[:, :, None]
    peer_w = swap(own_w.reshape(local, slots)).reshape(local, slots, 1)

    own, peer = [], []
    part = shard // CHUNKS
    for c in range(CHUNKS):
        gathered = lax.all_gather(
            out_grad[:, c * part : (c + 1) * part], "tensor", axis=1, tiled=True
        )
        outgoing = jnp.dot(placing, gathered, preferred_element_type=jnp.float32).astype(
            jnp.bfloat16
        )
        width = gathered.shape[1] // 2
        arrived = lax.all_to_all(
            outgoing.reshape(experts, capacity * local, 2 * width), "expert", 0, 0, tiled=True
        ).reshape(slots, local, 2 * width)
        theirs = lax.dynamic_slice_in_dim(arrived, (1 - dp_index) * width, width, 2)
        peer.append(swap(theirs.transpose(1, 0, 2)))
        mine = lax.dynamic_slice_in_dim(arrived, dp_index * width, width, 2)
        own.append(mine.transpose(1, 0, 2))

    sent = jax.ShapeDtypeStruct((local, slots, units), jnp.bfloat16)
    flops = 4 * local * slots * units * half
    rows = pltpu.VMEM((2 * slots, half), jnp.bfloat16)
    own_part, peer_part, partial = call(
        functools.partial(backprop_kernel, CHUNKS, tensor // 2),
        [*own, *peer, own_w, peer_w, hidden_act, peer_h, down_weight],
        [sent, sent, jax.ShapeDtypeStruct((local, 2 * slots, 1), jnp.float32)],
        [rows],
        flops,
    )
    come = swap(peer_part)

    every = lax.all_gather(partial.reshape(local, 2, slots), ("expert", "tensor", "dp"), axis=0)
    every = every.reshape(experts, tensor, 2, local, 2, experts, capacity)
    mine = lax.dynamic_index_in_dim(every, lax.axis_index("expert"), 5, keepdims=False)
    direct = lax.dynamic_index_in_dim(mine, dp_index, 2, keepdims=False)[:, :, :, 0]
    across = lax.dynamic_index_in_dim(mine, 1 - dp_index, 2, keepdims=False)[:, :, :, 1]
    scores = jnp.sum(direct + across, axis=1).transpose(0, 2, 1).reshape(-1)
    picked = jnp.sum(jnp.where(hit, scores[:, None], 0.0), axis=0)
    gate_grad = (picked * kept_mask).reshape(token_count, 2)

    (grad_down,) = call(
        functools.partial(grad_kernel, CHUNKS, tensor // 2),
        [*own, *peer, own_w, peer_w, hidden_act, peer_h],
        [jax.ShapeDtypeStruct(down_weight.shape, jnp.bfloat16)],
        [rows, pltpu.VMEM((2 * slots, units), jnp.bfloat16)],
        flops,
    )
    grad_hidden = (own_part.astype(jnp.float32) + come.astype(jnp.float32)).astype(jnp.bfloat16)
    return (grad_down, grad_hidden, gate_grad)


def solution(mesh):
    in_specs = (
        P(("expert", "dp"), "tensor"),
        P(("expert", "dp"), None),
        P(("expert", "dp"), None),
        P(("expert", "dp"), None),
        P("expert", "dp", "tensor"),
        P("expert", "tensor", "dp"),
    )
    out_specs = (
        P("expert", "tensor", "dp"),
        P("expert", "dp", "tensor"),
        P(("expert", "dp"), None),
    )
    return jax.shard_map(body, mesh=mesh, in_specs=in_specs, out_specs=out_specs, check_vma=False)
```

time: 336 us -> 243 us (0.72)
  matrix products: 76.5 us -> 5.79 us
  local copies, waits for them, and re-layouts: 82.3 us -> 15.1 us
  Pallas kernels: 0 us -> 43.5 us
  other arithmetic: 45 us -> 9.78 us
  blocking collectives: 16.9 us -> 47.3 us
  waiting for transfers between devices: 85.6 us -> 101 us
  starting transfers between devices: 14 us -> 5.53 us
    dot_general x5 -> x1, matrix products: 76.5 us -> 5.79 us  [body(): jnp.dot(placing, gathered, preferred_element_type=jnp.float32)]
    pallas_call x0 -> x2, Pallas kernels: none -> 43.5 us  [call(): pl.pallas_call(kernel, grid=(inputs[0].shape[0],), in_specs=[per_expert(a...]
    all_gather x0 -> x1, blocking collectives: none -> 40.1 us  [body(): lax.all_gather(partial.reshape(local, 2, slots), ('expert', 'tensor', 'dp...]
    unnamed x17 -> x12, local copies, waits for them, and re-layouts: 40.7 us -> 7.23 us
    convert_element_type x5 -> x2, other arithmetic: 35 us -> 5.2 us  [the longest x1 5.17 us: body(): (own_part.astype(jnp.float32) + come.astype(jnp.float32)).astype(jnp.bflo...]
    reshape x7 -> x3, local copies, waits for them, and re-layouts: 26.4 us -> 1.73 us  [the longest x1 1.11 us: body(): peer_w = swap(own_w.reshape(local, slots)).reshape(local, slots, 1)]
    psum x1 -> x0, blocking collectives: 16.9 us -> none  [body(): scores = lax.psum(partial_score, 'tensor')]
    all_gather x2 -> x1, waiting for transfers between devices: 32.1 us -> 47.1 us  [body(): lax.all_gather(out_grad[:, c * part:(c + 1) * part], 'tensor', axis=1, ti...]
  transfers between devices with their start and end apart: 7 -> 6, of which waited for: 2 -> 3; matrix products, arithmetic and copies ran while one was open for 47% -> 8% of each run, Pallas kernels for 0% -> 9%
where the time goes in v1:
time: 243 us; the launch traced here: 242 us
  waiting for transfers between devices  101 us (42%)
  blocking collectives  47.3 us (19%)
  Pallas kernels  43.5 us (18%)
  local copies, waits for them, and re-layouts  15.1 us (6%)
  between operations  14.2 us (6%)
  other arithmetic  9.78 us (4%)
  matrix products  5.79 us (2%)
  starting transfers between devices  5.53 us (2%)
    all_to_all x1, waiting for transfers between devices, body(): lax.all_to_all(outgoing.reshape(experts, capacity * local, 2 * width), 'e...  53.2 us
    all_gather x1, waiting for transfers between devices, body(): lax.all_gather(out_grad[:, c * part:(c + 1) * part], 'tensor', axis=1, ti...  47.1 us
    pallas_call x2, Pallas kernels, call(): pl.pallas_call(kernel, grid=(inputs[0].shape[0],), in_specs=[per_expert(a...  43.5 us
    all_gather x1, blocking collectives, body(): lax.all_gather(partial.reshape(local, 2, slots), ('expert', 'tensor', 'dp...  40.1 us
    unnamed x12, local copies, waits for them, and re-layouts  7.23 us
    all_to_all x1, blocking collectives, body(): lax.all_to_all(slot_scale.reshape(experts, capacity * local), 'expert', 0...  7.22 us
    dot_general x1, matrix products, body(): jnp.dot(placing, gathered, preferred_element_type=jnp.float32)  5.79 us
    convert_element_type x1, other arithmetic, body(): (own_part.astype(jnp.float32) + come.astype(jnp.float32)).astype(jnp.bflo...  5.17 us
  transfers between devices with their start and end apart: 6, of which 3 were waited for; matrix products, arithmetic and copies ran while one was open for 8% of the time, Pallas kernels for 9%

profile of v1, /device:TPU:0, one launch (start us, length us, event | category | flops | bytes accessed | tf_op | source)
XLA Modules:
  0.0 242.3 jit_solution(11546925225320941049)
XLA Ops:
  7.2 0.7 all-gather.2.cloned.1.call-update
  7.9 0.8 copy.69
  8.7 0.7 broadcast_compare_fusion
  9.4 0.2 copy.74
  9.6 0.2 eq.61
  9.8 0.5 convert_reduce_fusion
  10.3 0.2 mul.48
  10.5 0.3 fusion.7
  10.8 0.3 slice_reduce_fusion.1
  11.1 47.1 %all-gather.2.cloned.1.call-done = bf16[512,2048]{1,0:T(8,128)(2,1)} async-done(((bf16[512,512]{1,0:T(8,128)(2,1)}), bf16[512,2048]{1,0:T(8,128)(2,1)}) %all-gather.2.cloned.1.call-update) | async-done | bytes 2097168 | tf_op jit(solution)/shard_map/all_gather | solution.py:115
  58.2 5.8 %convolution_convert_fusion = bf16[1152,2048]{1,0:T(8,128)(2,1)} fusion(bf16[512,2048]{1,0:T(8,128)(2,1)} %all-gather.2.cloned.1.call-done, s32[512]{0:T(512)S(1)} %get-tuple-element.22, s32[512]{0:T(512)S(1)} %get-tuple-element.21), kind=kOutput, calls=%fused_computation.1 | convolution fusion | flops 2420047872 | bytes 6819840 | tf_op jit(solution)/shard_map/dot_general | solution.py:118
  64.0 4.9 %all-to-all-start = ((bf16[4,288,2048]{2,1,0:T(8,128)(2,1)}), bf16[4,288,2048]{2,1,0:T(8,128)(2,1)}, u32[]{:S(2)}, u32[]{:S(2)}) async-start(bf16[4,288,2048]{2,1,0:T(8,128)(2,1)} %bitcast.23), calls=%async_computation | async-start | bytes 9437184 | tf_op jit(solution)/shard_map/all_to_all | solution.py:122
  69.1 53.2 %all-to-all-done = bf16[4,288,2048]{2,1,0:T(8,128)(2,1)} async-done(((bf16[4,288,2048]{2,1,0:T(8,128)(2,1)}), bf16[4,288,2048]{2,1,0:T(8,128)(2,1)}, u32[]{:S(2)}, u32[]{:S(2)}) %all-to-all-start) | async-done | bytes 4718624 | tf_op jit(solution)/shard_map/all_to_all | solution.py:122
  122.2 2.9 %constant_dynamic-slice_fusion.2 = (bf16[144,8,1024]{2,1,0:T(8,128)(2,1)S(1)}, bf16[144,8,1024]{2,1,0:T(8,128)(2,1)S(1)}) fusion(bf16[144,8,2048]{2,1,0:T(8,128)(2,1)} %bitcast.1, s32[]{:T(128)S(6)} %select_n.60, s32[]{:T(128)S(6)} %select_n.59), kind=kLoop, calls=%fused_computation.54 | loop fusion | bytes 9437192 | tf_op jit(solution)/shard_map/dynamic_slice | solution.py:125
  125.1 2.7 %copy.111 = bf16[144,8,1024]{2,0,1:T(8,128)(2,1)} copy(bf16[144,8,1024]{2,1,0:T(8,128)(2,1)S(1)} %get-tuple-element.23) | data formatting | bytes 4718592
  128.2 0.2 reshape.121
  128.4 0.6 select_reduce_fusion.1
  129.0 7.2 %all_to_all.14 = f32[4,1,288]{2,1,0:T(1,128)S(1)} all-to-all(f32[4,1,288]{2,1,0:T(1,128)S(1)} %all_to_all.10), channel_id=1, replica_groups=mesh['expert'=4,'tensor'=4,'dp'=2] {'expert'}, dimensions={0} | all-to-all | bytes 9216 | tf_op jit(solution)/shard_map/all_to_all | solution.py:106
  136.5 1.1 copy.83.refs_2_
  137.7 1.1 copy.84.refs_3_
  138.9 2.7 %copy.112 = bf16[144,8,1024]{2,0,1:T(8,128)(2,1)} copy(bf16[144,8,1024]{2,1,0:T(8,128)(2,1)S(1)} %get-tuple-element.24) | data formatting | bytes 4718592
  141.6 20.8 %shard_map.86 = (bf16[8,144,1792]{2,1,0:T(8,128)(2,1)}, bf16[8,144,1792]{2,1,0:T(8,128)(2,1)}, f32[8,288,1]{2,1,0:T(8,128)}) custom-call(bf16[8,144,1024]{2,1,0:T(8,128)(2,1)} %bitcast.21, bf16[8,144,1024]{2,1,0:T(8,128)(2,1)} %collective-permute-done.refs_1_, f32[8,144,1]{2,1,0:T(8,128)} %copy.83.refs_2_, f32[8,144,1]{2,1,0:T(8,128)} %copy.84.refs_3_, ...), custom_call_target="tpu_custom_call" | custom-call | flops 8455716864 | bytes 50612224 | tf_op jit(solution)/shard_map/pallas_call | solution.py:69
  162.4 0.4 collective-permute-start.3
  162.8 1.7 reduce.4
  164.6 40.1 %all_gather.7 = f32[32,8,2,144]{3,1,2,0:T(8,128)S(1)} all-gather(f32[1,8,2,144]{3,1,2,0:T(8,128)S(1)} %copy.87), channel_id=1, replica_groups=mesh['expert'=4,'tensor'=4,'dp'=2] {'expert','tensor','dp'}, dimensions={0}, use_global_device_ids=true | all-gather | bytes 304128 | tf_op jit(solution)/shard_map/all_gather | solution.py:142
  204.7 0.5 reshape.120
  205.2 0.3 constant_dynamic-slice_fusion.1
  206.0 0.6 select_reduce_fusion
  206.6 0.2 reduce_sum.42
  206.9 0.7 copy.91
  207.6 22.7 %shard_map.85 = bf16[8,1792,1024]{2,1,0:T(8,128)(2,1)} custom-call(bf16[8,144,1024]{2,1,0:T(8,128)(2,1)} %bitcast.22, bf16[8,144,1024]{2,1,0:T(8,128)(2,1)} %collective-permute-done.refs_1_, f32[8,144,1]{2,1,0:T(8,128)} %copy.83.refs_2_, f32[8,144,1]{2,1,0:T(8,128)} %copy.84.refs_3_, bf16[8,144,1792]{2,1,0:T(8,128)(2,1)} %refs_4_.3, ...), custom_call_target="tpu_custom_call" | custom-call | flops 8455716864 | bytes 42345472 | tf_op jit(solution)/shard_map/pallas_call | solution.py:69
  230.3 5.2 %add_convert_fusion = bf16[8,144,1792]{2,1,0:T(8,128)(2,1)} fusion(bf16[8,144,1792]{2,1,0:T(8,128)(2,1)} %collective-permute-done.3, bf16[8,144,1792]{2,1,0:T(8,128)(2,1)S(1)} %copy-done), kind=kLoop, calls=%fused_computation | loop fusion | flops 8257536 | bytes 12386304 | tf_op jit(solution)/shard_map/convert_element_type | solution.py:158
  (30 shorter events, 1.6 us)
Async XLA Ops:
  7.2 51.1 %all-gather.2.cloned.1.call-start = ((), (), s32[]{:S(2)}) async-start(), calls=%async_computation.2 | async-start | bytes 2621440 | tf_op jit(solution)/shard_map/all_gather | solution.py:115
  64.0 58.2 %all-to-all-start = ((bf16[4,288,2048]{2,1,0:T(8,128)(2,1)}), bf16[4,288,2048]{2,1,0:T(8,128)(2,1)}, u32[]{:S(2)}, u32[]{:S(2)}) async-start(bf16[4,288,2048]{2,1,0:T(8,128)(2,1)} %bitcast.23), calls=%async_computation | async-start | bytes 9437184 | tf_op jit(solution)/shard_map/all_to_all | solution.py:122
  69.0 72.6 %collective-permute-start.2 = (bf16[8,144,1792]{2,1,0:T(8,128)(2,1)}, bf16[8,144,1792]{2,1,0:T(8,128)(2,1)}, u32[]{:S(2)}, u32[]{:S(2)}) collective-permute-start(bf16[8,144,1792]{2,1,0:T(8,128)(2,1)} %refs_4_.3), channel_id=1, source_target_pairs={{0,1},{1,0},{2,3},{3,2},{4,5},{5,4},{6,7},{7,6},{8,9},{9,8},{10,11... | collective-permute-start | bytes 12386312 | tf_op jit(solution)/shard_map/ppermute | solution.py:15
  125.1 2.7 %copy-start.1 = (s32[512,2]{0,1:T(2,128)S(1)}, s32[512,2]{0,1:T(2,128)}, u32[]{:S(2)}) copy-start(s32[512,2]{0,1:T(2,128)} %param.9) | copy-start | bytes 12292
  125.1 2.9 %copy-start.2 = (f32[512,2]{0,1:T(2,128)S(1)}, f32[512,2]{0,1:T(2,128)}, u32[]{:S(2)}) copy-start(f32[512,2]{0,1:T(2,128)} %param.8) | copy-start | bytes 12292
  127.8 13.7 %collective-permute-start = (bf16[8,144,1024]{2,1,0:T(8,128)(2,1)}, bf16[8,144,1024]{2,1,0:T(8,128)(2,1)}, u32[]{:S(2)}, u32[]{:S(2)}) collective-permute-start(bf16[8,144,1024]{2,1,0:T(8,128)(2,1)} %bitcast.19), channel_id=1, source_target_pairs={{0,1},{1,0},{2,3},{3,2},{4,5},{5,4},{6,7},{7,6},{8,9},{9,8},{10,11... | collective-permute-start | bytes 7077896 | tf_op jit(solution)/shard_map/ppermute | solution.py:15
  136.4 1.3 collective-permute-start.1
  162.4 67.9 %collective-permute-start.3 = (bf16[8,144,1792]{2,1,0:T(8,128)(2,1)}, bf16[8,144,1792]{2,1,0:T(8,128)(2,1)}, u32[]{:S(2)}, u32[]{:S(2)}) collective-permute-start(bf16[8,144,1792]{2,1,0:T(8,128)(2,1)} %get-tuple-element.7), channel_id=1, source_target_pairs={{0,1},{1,0},{2,3},{3,2},{4,5},{5,4},{6,7},{7,6},{8,9},{9,8},{10,11... | collective-permute-start | bytes 12386312 | tf_op jit(solution)/shard_map/ppermute | solution.py:15
  207.6 22.7 %copy-start = (bf16[8,144,1792]{2,1,0:T(8,128)(2,1)S(1)}, bf16[8,144,1792]{2,1,0:T(8,128)(2,1)}, u32[]{:S(2)}) copy-start(bf16[8,144,1792]{2,1,0:T(8,128)(2,1)} %get-tuple-element.6) | copy-start | bytes 12386308
Sparse Core Ops, SparseCore 0:
  9.6 48.6 all-gather.1

commit v2 on v1

--- a/solution.py
+++ b/solution.py
@@ -7,7 +7,7 @@
 from jax.experimental.pallas import tpu as pltpu
 from jax.sharding import PartitionSpec as P
 
-CHUNKS = 1
+CHUNKS = 2
 VMEM_LIMIT = 56 * 1024 * 1024
 
 
@@ -139,12 +139,13 @@
     )
     come = swap(peer_part)
 
-    every = lax.all_gather(partial.reshape(local, 2, slots), ("expert", "tensor", "dp"), axis=0)
-    every = every.reshape(experts, tensor, 2, local, 2, experts, capacity)
-    mine = lax.dynamic_index_in_dim(every, lax.axis_index("expert"), 5, keepdims=False)
-    direct = lax.dynamic_index_in_dim(mine, dp_index, 2, keepdims=False)[:, :, :, 0]
-    across = lax.dynamic_index_in_dim(mine, 1 - dp_index, 2, keepdims=False)[:, :, :, 1]
-    scores = jnp.sum(direct + across, axis=1).transpose(0, 2, 1).reshape(-1)
+    partial = partial.reshape(local, 2, slots)
+    partial = lax.psum(jnp.where(dp_index == 0, partial, partial[:, ::-1]), ("tensor", "dp"))
+    mine = lax.dynamic_index_in_dim(partial, dp_index, 1, keepdims=False)
+    mine = mine.reshape(local, experts, capacity).transpose(1, 2, 0)
+    scores = lax.all_to_all(
+        mine.reshape(experts, capacity * local), "expert", 0, 0, tiled=True
+    ).reshape(-1)
     picked = jnp.sum(jnp.where(hit, scores[:, None], 0.0), axis=0)
     gate_grad = (picked * kept_mask).reshape(token_count, 2)
 

time: 243 us -> 233 us (0.959)
  waiting for transfers between devices: 101 us -> 80.7 us
  blocking collectives: 47.3 us -> 34.6 us
  local copies, waits for them, and re-layouts: 15.1 us -> 24.3 us
  starting transfers between devices: 5.53 us -> 12.7 us
  other arithmetic: 9.78 us -> 13.3 us
    all_gather x1 -> x0, blocking collectives: 40.1 us -> none  [body(): lax.all_gather(partial.reshape(local, 2, slots), ('expert', 'tensor', 'dp...]
    psum x0 -> x1, blocking collectives: none -> 26.8 us  [body(): lax.psum(jnp.where(dp_index == 0, partial, partial[:, ::-1]), ('tensor',...]
    all_to_all x1 -> x2, waiting for transfers between devices: 53.2 us -> 27 us  [body(): lax.all_to_all(outgoing.reshape(experts, capacity * local, 2 * width), 'e...]
    all_gather x1 -> x2, waiting for transfers between devices: 47.1 us -> 52.9 us  [body(): lax.all_gather(out_grad[:, c * part:(c + 1) * part], 'tensor', axis=1, ti...]
    all_to_all x0 -> x1, starting transfers between devices: none -> 3.38 us  [body(): lax.all_to_all(mine.reshape(experts, capacity * local), 'expert', 0, 0, t...]
    all_to_all x1 -> x2, starting transfers between devices: 4.93 us -> 8.14 us  [body(): lax.all_to_all(outgoing.reshape(experts, capacity * local, 2 * width), 'e...]
    unnamed x12 -> x18, local copies, waits for them, and re-layouts: 7.23 us -> 9.74 us
    dot_general x1 -> x2, matrix products: 5.79 us -> 8.06 us  [body(): jnp.dot(placing, gathered, preferred_element_type=jnp.float32)]
  transfers between devices with their start and end apart: 6 -> 10, of which waited for: 3 -> 3; matrix products, arithmetic and copies ran while one was open for 8% -> 15% of each run, Pallas kernels for 9% -> 10%
where the time goes in v2:
time: 233 us; the launch traced here: 232 us
  waiting for transfers between devices  80.7 us (35%)
  Pallas kernels  43.8 us (19%)
  blocking collectives  34.6 us (15%)
  local copies, waits for them, and re-layouts  24.3 us (10%)
  between operations  14.2 us (6%)
  other arithmetic  13.3 us (6%)
  starting transfers between devices  12.7 us (5%)
  matrix products  8.06 us (3%)
    all_gather x2, waiting for transfers between devices, body(): lax.all_gather(out_grad[:, c * part:(c + 1) * part], 'tensor', axis=1, ti...  52.9 us
    pallas_call x2, Pallas kernels, call(): pl.pallas_call(kernel, grid=(inputs[0].shape[0],), in_specs=[per_expert(a...  43.8 us
    all_to_all x2, waiting for transfers between devices, body(): lax.all_to_all(outgoing.reshape(experts, capacity * local, 2 * width), 'e...  27 us
    psum x1, blocking collectives, body(): lax.psum(jnp.where(dp_index == 0, partial, partial[:, ::-1]), ('tensor',...  26.8 us
    unnamed x18, local copies, waits for them, and re-layouts  9.74 us
    all_to_all x2, starting transfers between devices, body(): lax.all_to_all(outgoing.reshape(experts, capacity * local, 2 * width), 'e...  8.14 us
    dot_general x2, matrix products, body(): jnp.dot(placing, gathered, preferred_element_type=jnp.float32)  8.06 us
    all_to_all x1, blocking collectives, body(): lax.all_to_all(slot_scale.reshape(experts, capacity * local), 'expert', 0...  7.84 us
  transfers between devices with their start and end apart: 10, of which 3 were waited for; matrix products, arithmetic and copies ran while one was open for 15% of the time, Pallas kernels for 10%

profile of v2, /device:TPU:0, one launch (start us, length us, event | category | flops | bytes accessed | tf_op | source)
XLA Modules:
  0.0 231.7 jit_solution(8958554102103627246)
XLA Ops:
  7.2 1.9 fusion.23
  10.5 0.8 copy.74
  13.1 30.0 %all-gather.3.cloned.1.call-done = bf16[512,1024]{1,0:T(8,128)(2,1)} async-done(((bf16[512,256]{1,0:T(8,128)(2,1)}), bf16[512,1024]{1,0:T(8,128)(2,1)}) %all-gather.3.cloned.1.call-update) | async-done | bytes 1048592 | tf_op jit(solution)/shard_map/all_gather | solution.py:115
  43.1 4.0 %convolution_convert_fusion.1 = bf16[1152,1024]{1,0:T(8,128)(2,1)} fusion(bf16[512,1024]{1,0:T(8,128)(2,1)} %all-gather.3.cloned.1.call-done, s32[512]{0:T(512)S(1)} %get-tuple-element.22, s32[512]{0:T(512)S(1)} %get-tuple-element.21), kind=kOutput, calls=%fused_computation.8 | convolution fusion | flops 1210908672 | bytes 3411968 | tf_op jit(solution)/shard_map/dot_general | solution.py:118
  47.1 3.6 %all-to-all-start = ((bf16[4,288,1024]{2,1,0:T(8,128)(2,1)}), bf16[4,288,1024]{2,1,0:T(8,128)(2,1)S(1)}, u32[]{:S(2)}, u32[]{:S(2)}) async-start(bf16[4,288,1024]{2,1,0:T(8,128)(2,1)} %bitcast.31), calls=%async_computation | async-start | bytes 4718592 | tf_op jit(solution)/shard_map/all_to_all | solution.py:122
  50.8 22.9 %all-gather.5.cloned.1.call-done = bf16[512,1024]{1,0:T(8,128)(2,1)} async-done(((bf16[512,256]{1,0:T(8,128)(2,1)}), bf16[512,1024]{1,0:T(8,128)(2,1)}) %all-gather.5.cloned.1.call-update) | async-done | bytes 1048592 | tf_op jit(solution)/shard_map/all_gather | solution.py:115
  73.7 4.0 %convolution_convert_fusion = bf16[1152,1024]{1,0:T(8,128)(2,1)} fusion(bf16[512,1024]{1,0:T(8,128)(2,1)} %all-gather.5.cloned.1.call-done, s32[512]{0:T(512)S(1)} %get-tuple-element.22, s32[512]{0:T(512)S(1)} %get-tuple-element.21), kind=kOutput, calls=%fused_computation.7 | convolution fusion | flops 1210908672 | bytes 3411968 | tf_op jit(solution)/shard_map/dot_general | solution.py:118
  77.8 4.5 %all-to-all-start.1 = ((bf16[4,288,1024]{2,1,0:T(8,128)(2,1)}), bf16[4,288,1024]{2,1,0:T(8,128)(2,1)}, u32[]{:S(2)}, u32[]{:S(2)}) async-start(bf16[4,288,1024]{2,1,0:T(8,128)(2,1)} %bitcast.30), calls=%async_computation.1 | async-start | bytes 4718592 | tf_op jit(solution)/shard_map/all_to_all | solution.py:122
  82.3 27.0 %all-to-all-done.1 = bf16[4,288,1024]{2,1,0:T(8,128)(2,1)} async-done(((bf16[4,288,1024]{2,1,0:T(8,128)(2,1)}), bf16[4,288,1024]{2,1,0:T(8,128)(2,1)}, u32[]{:S(2)}, u32[]{:S(2)}) %all-to-all-start.1) | async-done | bytes 2359328 | tf_op jit(solution)/shard_map/all_to_all | solution.py:122
  109.3 3.1 %constant_dynamic-slice_fusion = (bf16[144,8,512]{2,1,0:T(8,128)(2,1)S(1)}, bf16[144,8,512]{2,1,0:T(8,128)(2,1)}, bf16[144,8,512]{2,1,0:T(8,128)(2,1)S(1)}, bf16[144,8,512]{2,1,0:T(8,128)(2,1)S(1)}) fusion(bf16[144,8,1024]{2,1,0:T(8,128)(2,1)} %bitcast.4, s32[]{:T(128)S(6)} %select_n.57, s32[]{:T(128)S(6)} %select_n.56, bf16[144,8,1024]{2,1,0:T(8,128)(2,1)S(1)} %bitcast.29), kind=kLoop, calls=%fused_computation.55 | loop fusion | bytes 9437192 | tf_op jit(solution)/shard_map/dynamic_slice | solution.py:125
  112.4 1.4 copy.115
  113.8 1.4 copy.116
  115.7 0.9 copy.86
  116.5 0.9 copy.87
  117.4 1.8 fusion.15
  119.1 1.1 reshape.134
  121.5 7.8 %all_to_all.29 = f32[4,1,288]{2,1,0:T(1,128)S(1)} all-to-all(f32[4,1,288]{2,1,0:T(1,128)} %all_to_all.20), channel_id=1, replica_groups=mesh['expert'=4,'tensor'=4,'dp'=2] {'expert'}, dimensions={0} | all-to-all | bytes 9216 | tf_op jit(solution)/shard_map/all_to_all | solution.py:106
  130.0 1.4 reshape.130
  131.4 0.9 copy.88
  132.4 1.1 copy.90.refs_4_
  133.5 0.9 copy.89
  134.4 1.1 copy.91.refs_5_
  135.5 1.4 copy.117
  136.9 1.4 copy.118
  138.3 1.0 copy-done.1
  139.3 20.9 %shard_map.86 = (bf16[8,144,1792]{2,1,0:T(8,128)(2,1)}, bf16[8,144,1792]{2,1,0:T(8,128)(2,1)}, f32[8,288,1]{2,1,0:T(8,128)}) custom-call(bf16[8,144,512]{2,1,0:T(8,128)(2,1)} %bitcast.27, bf16[8,144,512]{2,1,0:T(8,128)(2,1)} %bitcast.25, bf16[8,144,512]{2,1,0:T(8,128)(2,1)} %copy-done.1, bf16[8,144,512]{2,1,0:T(8,128)(2,1)} %collective-permute-done.1.refs_3_, ...), custom_call_target="tpu_custom_call" | custom-call | flops 8455716864 | bytes 50612224 | tf_op jit(solution)/shard_map/pallas_call | solution.py:69
  160.7 1.7 reduce.3
  162.7 26.8 %psum.7 = f32[8,2,144]{2,1,0:T(2,128)S(1)} all-reduce(f32[8,2,144]{2,1,0:T(2,128)S(1)} %bitcast.35), channel_id=1, replica_groups=mesh['expert'=4,'tensor'=4,'dp'=2] {'tensor','dp'}, use_global_device_ids=true, to_apply=%region_2.3 | all-reduce | flops 2304 | bytes 18432 | tf_op jit(solution)/shard_map/psum | solution.py:143
  190.4 3.4 %all-to-all-start.3 = ((f32[4,1,288]{2,1,0:T(1,128)}), f32[4,1,288]{2,1,0:T(1,128)S(1)}, u32[]{:S(2)}, u32[]{:S(2)}) async-start(f32[4,1,288]{2,1,0:T(1,128)} %all_to_all.24), calls=%async_computation.3 | async-start | bytes 12288 | tf_op jit(solution)/shard_map/all_to_all | solution.py:146
  193.8 23.0 %shard_map.85 = bf16[8,1792,1024]{2,1,0:T(8,128)(2,1)} custom-call(bf16[8,144,512]{2,1,0:T(8,128)(2,1)} %bitcast.28, bf16[8,144,512]{2,1,0:T(8,128)(2,1)} %bitcast.26, bf16[8,144,512]{2,1,0:T(8,128)(2,1)} %copy-done.1, bf16[8,144,512]{2,1,0:T(8,128)(2,1)} %collective-permute-done.1.refs_3_, f32[8,144,1]{2,1,0:T(8,128)} %copy.90.refs_4_, ...), custom_call_target="tpu_custom_call" | custom-call | flops 8455716864 | bytes 42345472 | tf_op jit(solution)/shard_map/pallas_call | solution.py:69
  217.7 0.7 copy.96
  218.4 6.4 %add_convert_fusion = bf16[8,144,1792]{2,1,0:T(8,128)(2,1)} fusion(bf16[8,144,1792]{2,1,0:T(8,128)(2,1)} %collective-permute-done.4, bf16[8,144,1792]{2,1,0:T(8,128)(2,1)} %get-tuple-element.6), kind=kLoop, calls=%fused_computation | loop fusion | flops 8257536 | bytes 12386304 | tf_op jit(solution)/shard_map/convert_element_type | solution.py:159
  (48 shorter events, 8.2 us)
Async XLA Ops:
  7.2 35.9 %all-gather.3.cloned.1.call-start = ((), (), s32[]{:S(2)}) async-start(), calls=%async_computation.4 | async-start | bytes 1310720 | tf_op jit(solution)/shard_map/all_gather | solution.py:115
  9.1 64.7 %all-gather.5.cloned.1.call-start = ((), (), s32[]{:S(2)}) async-start(), calls=%async_computation.5 | async-start | bytes 1310720 | tf_op jit(solution)/shard_map/all_gather | solution.py:115
  47.1 30.7 %all-to-all-start = ((bf16[4,288,1024]{2,1,0:T(8,128)(2,1)}), bf16[4,288,1024]{2,1,0:T(8,128)(2,1)S(1)}, u32[]{:S(2)}, u32[]{:S(2)}) async-start(bf16[4,288,1024]{2,1,0:T(8,128)(2,1)} %bitcast.31), calls=%async_computation | async-start | bytes 4718592 | tf_op jit(solution)/shard_map/all_to_all | solution.py:122
  50.8 87.5 %collective-permute-start.3 = (bf16[8,144,1792]{2,1,0:T(8,128)(2,1)}, bf16[8,144,1792]{2,1,0:T(8,128)(2,1)}, u32[]{:S(2)}, u32[]{:S(2)}) collective-permute-start(bf16[8,144,1792]{2,1,0:T(8,128)(2,1)} %refs_6_.3), channel_id=1, source_target_pairs={{0,1},{1,0},{2,3},{3,2},{4,5},{5,4},{6,7},{7,6},{8,9},{9,8},{10,11... | collective-permute-start | bytes 12386312 | tf_op jit(solution)/shard_map/ppermute | solution.py:15
  77.8 31.5 %all-to-all-start.1 = ((bf16[4,288,1024]{2,1,0:T(8,128)(2,1)}), bf16[4,288,1024]{2,1,0:T(8,128)(2,1)}, u32[]{:S(2)}, u32[]{:S(2)}) async-start(bf16[4,288,1024]{2,1,0:T(8,128)(2,1)} %bitcast.30), calls=%async_computation.1 | async-start | bytes 4718592 | tf_op jit(solution)/shard_map/all_to_all | solution.py:122
  112.4 3.3 %copy-start.3 = (s32[512,2]{0,1:T(2,128)S(1)}, s32[512,2]{0,1:T(2,128)}, u32[]{:S(2)}) copy-start(s32[512,2]{0,1:T(2,128)} %param.9) | copy-start | bytes 12292
  112.4 4.1 %copy-start.4 = (f32[512,2]{0,1:T(2,128)S(1)}, f32[512,2]{0,1:T(2,128)}, u32[]{:S(2)}) copy-start(f32[512,2]{0,1:T(2,128)} %param.8) | copy-start | bytes 12292
  113.8 21.7 %copy-start = (bf16[144,8,512]{2,1,0:T(8,128)(2,1)S(1)}, bf16[144,8,512]{2,1,0:T(8,128)(2,1)}, u32[]{:S(2)}) copy-start(bf16[144,8,512]{2,1,0:T(8,128)(2,1)} %get-tuple-element.24) | copy-start | bytes 3538948
  115.2 23.1 %collective-permute-start = (bf16[8,144,512]{2,1,0:T(8,128)(2,1)}, bf16[8,144,512]{2,1,0:T(8,128)(2,1)S(1)}, u32[]{:S(2)}, u32[]{:S(2)}) collective-permute-start(bf16[8,144,512]{2,1,0:T(8,128)(2,1)} %bitcast.19), channel_id=1, source_target_pairs={{0,1},{1,0},{2,3},{3,2},{4,5},{5,4},{6,7},{7,6},{8,9},{9,8},{10,11... | collective-permute-start | bytes 3538952 | tf_op jit(solution)/shard_map/ppermute | solution.py:15
  115.2 23.1 %collective-permute-start.1 = (bf16[8,144,512]{2,1,0:T(8,128)(2,1)}, bf16[8,144,512]{2,1,0:T(8,128)(2,1)}, u32[]{:S(2)}, u32[]{:S(2)}) collective-permute-start(bf16[8,144,512]{2,1,0:T(8,128)(2,1)} %bitcast.18), channel_id=1, source_target_pairs={{0,1},{1,0},{2,3},{3,2},{4,5},{5,4},{6,7},{7,6},{8,9},{9,8},{10,11... | collective-permute-start | bytes 3538952 | tf_op jit(solution)/shard_map/ppermute | solution.py:15
  131.4 2.1 collective-permute-start.2
  138.3 1.0 copy-start.1
  160.2 58.2 %collective-permute-start.4 = (bf16[8,144,1792]{2,1,0:T(8,128)(2,1)}, bf16[8,144,1792]{2,1,0:T(8,128)(2,1)}, u32[]{:S(2)}, u32[]{:S(2)}) collective-permute-start(bf16[8,144,1792]{2,1,0:T(8,128)(2,1)} %get-tuple-element.7), channel_id=1, source_target_pairs={{0,1},{1,0},{2,3},{3,2},{4,5},{5,4},{6,7},{7,6},{8,9},{9,8},{10,11... | collective-permute-start | bytes 12386312 | tf_op jit(solution)/shard_map/ppermute | solution.py:15
  190.4 26.4 %all-to-all-start.3 = ((f32[4,1,288]{2,1,0:T(1,128)}), f32[4,1,288]{2,1,0:T(1,128)S(1)}, u32[]{:S(2)}, u32[]{:S(2)}) async-start(f32[4,1,288]{2,1,0:T(1,128)} %all_to_all.24), calls=%async_computation.3 | async-start | bytes 12288 | tf_op jit(solution)/shard_map/all_to_all | solution.py:146
  193.8 23.9 %copy-start.2 = (s32[512,2]{1,0:T(8,128)S(1)}, s32[512,2]{1,0:T(8,128)}, u32[]{:S(2)}) copy-start(s32[512,2]{1,0:T(8,128)} %copy.86) | copy-start | bytes 12292
Sparse Core Ops, SparseCore 0:
  10.1 32.8 all-gather.2
  45.2 28.4 all-gather.4
